TPU v7x, 32 devices: a whole 2x2x4 slice. The times are simulated.
32 devices in a mesh: dp: 4 (over y, core), tensor: 8 (over z, x).
Axes of the slice: x: 2, y: 2, z: 4, core: 2. Of those that a mesh axis runs over, the one named last changes fastest.
Arguments:
- gradient: bfloat16 [2048, 7168], P('dp', 'tensor'), may hold values from -8000 to 8000
- block_owner: int32 [56], replicated, may hold values from 0 to 63, as said below
- tile_block: int32 [4, 56], replicated, may hold values from 0 to 55, as said below
- fast_weight: float32 [2048, 7168], P('dp', 'tensor'), may hold values from -6 to 6
- slow_flat: float32 [2048, 7168], P(('dp', 'tensor')), may hold values from -6 to 6
- left_stat: float32 [64, 512, 512], P(('dp', 'tensor')), may hold values from -6 to 6
- right_stat: float32 [64, 512, 512], P(('dp', 'tensor')), may hold values from -6 to 6
- left_basis: bfloat16 [64, 512, 512], P(('dp', 'tensor')), may hold values from -0.25 to 0.25
- right_basis: bfloat16 [64, 512, 512], P(('dp', 'tensor')), may hold values from -0.25 to 0.25
- first_moment: float32 [64, 512, 512], P(('dp', 'tensor')), may hold values from -3 to 3
- second_moment: float32 [64, 512, 512], P(('dp', 'tensor')), may hold values from 0.05 to 0.5
Outputs:
- fast_new: float32 [2048, 7168], P('dp', 'tensor')
- slow_new: float32 [2048, 7168], P(('dp', 'tensor'))
- left_new: float32 [64, 512, 512], P(('dp', 'tensor'))
- right_new: float32 [64, 512, 512], P(('dp', 'tensor'))
- moment_new: float32 [64, 512, 512], P(('dp', 'tensor'))
- second_new: float32 [64, 512, 512], P(('dp', 'tensor'))
Inputs may be any that keep to these rules, and one draw needn't show every extreme that they name: `tile_block`: entry [r, g] is the number of the block that tile g of block row r (columns g * 128 to g * 128 + 127) belongs to, one of r * (14) to r * 14 + 7168 // 512 - 1. Each such block has 4 tiles, which lie in the columns of different tensor indices. In each row the tensor indices fall into groups of 4, and every block takes one tile from each member of one group. `block_owner`: entry b is the slot d * 2 + k of block b's owner, where d = (dp index) * (number of tensor indices) + (tensor index) and k is 0 or 1; the owner's dp index is the block's row. No slot is named twice, every device owns one or two blocks, and a device's two blocks come from different groups.
All inputs are finite; a program needn't handle non-finite values.
Results may differ from a plain program's by a relative error of at most 0.00095.
Values may be sent and summed in bfloat16 or wider, within the bound.
A program may use at most 128 MiB of HBM per device.

v0:
```python
import jax
import jax.numpy as jnp
from jax import lax
from jax.sharding import PartitionSpec as P

BETA_STAT = 0.95
BETA_ONE = 0.9
BETA_TWO = 0.95
ADAM_EPS = 1e-08
STEP_RATE = 0.1
PULL_RATE = 0.5
CLIP_RMS = 0.5
HIGHEST = lax.Precision.HIGHEST


def soap_block(
    grad_block, factor, left_stat, right_stat, left_basis, right_basis, first_moment, second_moment
):
    gram_left = jnp.dot(grad_block, grad_block.T, preferred_element_type=jnp.float32)
    gram_right = jnp.dot(grad_block.T, grad_block, preferred_element_type=jnp.float32)
    squared = factor * factor
    left_next = BETA_STAT * left_stat + (1.0 - BETA_STAT) * squared * gram_left
    right_next = BETA_STAT * right_stat + (1.0 - BETA_STAT) * squared * gram_right
    left_wide = left_basis.astype(jnp.float32)
    right_wide = right_basis.astype(jnp.float32)
    half_rotated = jnp.dot(left_basis.T, grad_block, preferred_element_type=jnp.float32)
    rotated = factor * jnp.dot(half_rotated, right_wide, precision=HIGHEST)
    moment_next = BETA_ONE * first_moment + (1.0 - BETA_ONE) * factor * grad_block.astype(
        jnp.float32
    )
    second_next = BETA_TWO * second_moment + (1.0 - BETA_TWO) * rotated * rotated
    moment_turned = jnp.dot(
        jnp.dot(left_wide.T, moment_next, precision=HIGHEST), right_wide, precision=HIGHEST
    )
    direction = moment_turned / (jnp.sqrt(second_next) + ADAM_EPS)
    update = jnp.dot(
        jnp.dot(left_wide, direction, precision=HIGHEST), right_wide.T, precision=HIGHEST
    )
    return (left_next, right_next, moment_next, second_next, update.astype(jnp.bfloat16))


def on_device(
    gradient,
    block_owner,
    tile_block,
    fast_weight,
    slow_flat,
    left_stat,
    right_stat,
    left_basis,
    right_basis,
    first_moment,
    second_moment,
):
    block_size = left_stat.shape[1]
    slot_count = left_stat.shape[0]
    row_count, shard_cols = gradient.shape
    tensor_size = lax.axis_size("tensor")
    column = lax.axis_index("tensor")
    dp_index = lax.axis_index("dp")
    tile_count = tile_block.shape[1]
    tile_width = shard_cols * tensor_size // tile_count
    shard_tiles = shard_cols // tile_width
    per_block = block_size // tile_width
    rows_flat = block_size // tensor_size
    total_count = row_count * shard_cols * lax.axis_size("dp") * tensor_size
    fast_ahead = lax.all_to_all(fast_weight, "tensor", split_axis=0, concat_axis=1, tiled=True)
    wide_grad = gradient.astype(jnp.float32)
    square_sum = lax.psum(jnp.sum(wide_grad * wide_grad), ("dp", "tensor"))
    factor = CLIP_RMS / jnp.sqrt(square_sum / total_count + 1e-06)
    numbers = jnp.arange(block_owner.shape[0], dtype=jnp.int32)
    peer_ids = jnp.arange(tensor_size, dtype=jnp.int32)
    positions = jnp.arange(per_block, dtype=jnp.int32)
    row_tiles = lax.dynamic_index_in_dim(tile_block, dp_index, 0, keepdims=False)
    peer_tiles = row_tiles.reshape(tensor_size, shard_tiles)
    my_blocks = lax.dynamic_index_in_dim(peer_tiles, column, 0, keepdims=False)
    owner_slot = jnp.sum(
        jnp.where(my_blocks[:, None] == numbers[None, :], block_owner[None, :], 0), axis=1
    )
    target = owner_slot // slot_count % tensor_size
    send_map = (peer_ids[:, None] == target[None, :]).astype(jnp.bfloat16)
    tile_view = gradient.reshape(row_count, shard_tiles, tile_width)
    outgoing = jnp.einsum(
        "pi,bit->pbt", send_map, tile_view, preferred_element_type=jnp.float32
    ).astype(jnp.bfloat16)
    arrived = lax.all_to_all(outgoing, "tensor", split_axis=0, concat_axis=0, tiled=True)
    slot_ids = (dp_index * tensor_size + column) * slot_count + jnp.arange(
        slot_count, dtype=jnp.int32
    )
    matches = block_owner[None, :] == slot_ids[:, None]
    present = jnp.any(matches, axis=1)
    owned_block = jnp.sum(jnp.where(matches, numbers[None, :], 0), axis=1)
    holders = (
        jnp.any(peer_tiles[None, :, :] == owned_block[:, None, None], axis=2) & present[:, None]
    )
    slot_rank = jnp.cumsum(holders.astype(jnp.int32), axis=1) - 1
    select = (holders[:, None, :] & (slot_rank[:, None, :] == positions[None, :, None])).astype(
        jnp.bfloat16
    )
    blocks = jnp.einsum(
        "kjp,pbt->kbjt", select, arrived, preferred_element_type=jnp.float32
    ).astype(jnp.bfloat16)
    blocks = blocks.reshape(slot_count, block_size, block_size)
    results = jax.vmap(soap_block, in_axes=(0, None, 0, 0, 0, 0, 0, 0))(
        blocks, factor, left_stat, right_stat, left_basis, right_basis, first_moment, second_moment
    )
    keep_mask = present[:, None, None]
    left_new = jnp.where(keep_mask, results[0], left_stat)
    right_new = jnp.where(keep_mask, results[1], right_stat)
    moment_new = jnp.where(keep_mask, results[2], first_moment)
    second_new = jnp.where(keep_mask, results[3], second_moment)
    update = jnp.where(keep_mask, results[4], jnp.zeros((), jnp.bfloat16))
    pieces = update.reshape(slot_count, block_size, per_block, tile_width)
    backward = jnp.einsum(
        "kjp,kbjt->pbt", select, pieces, preferred_element_type=jnp.float32
    ).astype(jnp.bfloat16)
    returned = lax.all_to_all(backward, "tensor", split_axis=0, concat_axis=0, tiled=True)
    home_update = jnp.einsum(
        "pi,pbt->bit", send_map, returned, preferred_element_type=jnp.float32
    ).reshape(row_count, shard_cols)
    fast_new = fast_weight - STEP_RATE * home_update
    rows_out = update.reshape(slot_count, tensor_size, rows_flat, block_size)
    arriving = lax.all_to_all(rows_out, "tensor", split_axis=1, concat_axis=1, tiled=True)
    source_slots = (dp_index * tensor_size + peer_ids[None, :]) * slot_count + jnp.arange(
        slot_count, dtype=jnp.int32
    )[:, None]
    found_slot = block_owner[None, None, :] == source_slots[:, :, None]
    source_has = jnp.any(found_slot, axis=2)
    source_block = jnp.sum(jnp.where(found_slot, numbers[None, None, :], 0), axis=2)
    tile_ids = jnp.arange(tile_count, dtype=jnp.int32)
    same_block = row_tiles[:, None] == row_tiles[None, :]
    tile_rank = jnp.sum(same_block & (tile_ids[None, :] < tile_ids[:, None]), axis=1)
    belongs = (row_tiles[:, None, None] == source_block[None, :, :]) & source_has[None, :, :]
    placing = (
        belongs[:, :, :, None] & (tile_rank[:, None, None, None] == positions[None, None, None, :])
    ).astype(jnp.bfloat16)
    received = arriving.reshape(slot_count, tensor_size, rows_flat, per_block, tile_width)
    flat_update = jnp.einsum(
        "gkpj,kprjt->rgt", placing, received, preferred_element_type=jnp.float32
    ).reshape(rows_flat, tile_count * tile_width)
    flat_fast = fast_ahead - STEP_RATE * flat_update
    slow_new = slow_flat + PULL_RATE * (flat_fast - slow_flat)
    return (fast_new, slow_new, left_new, right_new, moment_new, second_new)


def solution(mesh):
    placed = (
        P("dp", "tensor"),
        P(),
        P(),
        P("dp", "tensor"),
        P(("dp", "tensor"), None),
        P(("dp", "tensor"), None, None),
        P(("dp", "tensor"), None, None),
        P(("dp", "tensor"), None, None),
        P(("dp", "tensor"), None, None),
        P(("dp", "tensor"), None, None),
        P(("dp", "tensor"), None, None),
    )
    return jax.shard_map(
        on_device,
        mesh=mesh,
        in_specs=placed,
        out_specs=(
            P("dp", "tensor"),
            P(("dp", "tensor"), None),
            P(("dp", "tensor"), None, None),
            P(("dp", "tensor"), None, None),
            P(("dp", "tensor"), None, None),
            P(("dp", "tensor"), None, None),
        ),
        check_vma=False,
    )
```

profile of v0, /device:TPU:0, one launch (start us, length us, event | category | flops | bytes accessed | tf_op | source)
XLA Modules:
  0.0 172.0 jit_solution(6821880046149624700)
XLA Ops:
  0.7 0.8 fusion.43
  1.5 0.8 select_reduce_fusion
  2.4 1.5 copy.83
  3.9 0.8 copy.85
  4.6 0.6 convolution_convert_fusion.1
  5.2 1.1 copy.86
  6.4 7.3 %all-to-all-start = ((bf16[8,512,128]{2,1,0:T(8,128)(2,1)}), bf16[8,512,128]{2,1,0:T(8,128)(2,1)S(1)}, u32[]{:S(2)}, u32[]{:S(2)}) async-start(bf16[8,512,128]{2,1,0:T(8,128)(2,1)} %copy.86), calls=%async_computation | async-start | bytes 2097152 | tf_op jit(solution)/shard_map/all_to_all | solution.py:86
  13.6 1.1 multiply_reduce_fusion
  14.7 44.9 %psum.7 = f32[]{:T(128)} all-reduce(f32[]{:T(128)} %multiply_reduce_fusion), channel_id=1, replica_groups=mesh['dp'=4,'tensor'=8] {'dp','tensor'}, use_global_device_ids=true, to_apply=%region_5.6 | all-reduce | flops 1 | bytes 8 | tf_op jit(solution)/shard_map/psum | solution.py:69
  59.6 0.2 fusion.41
  59.8 0.2 compare_reduce_fusion.1
  60.0 0.2 compare_reduce_fusion.2
  60.3 0.2 reduce_window_sum.11
  61.2 5.3 %all-to-all-start.2 = ((f32[8,64,896]{2,1,0:T(8,128)}), f32[8,64,896]{2,1,0:T(8,128)}, u32[]{:S(2)}, u32[]{:S(2)}) async-start(f32[8,64,896]{2,1,0:T(8,128)} %bitcast.11), calls=%async_computation.2 | async-start | bytes 3670016 | tf_op jit(solution)/shard_map/all_to_all | solution.py:67
  66.5 0.9 fusion.10
  67.4 0.4 reshape.167
  67.9 1.6 copy.91
  69.5 2.4 %fusion.49 = f32[2,512,512]{1,2,0:T(8,128)S(1)} fusion(bf16[2,512,512]{1,2,0:T(8,128)(2,1)S(1)} %copy.91, bf16[2,512,512]{2,1,0:T(8,128)(2,1)} %param.18), kind=kOutput, calls=%fused_computation.86 | convolution fusion | flops 536870912 | bytes 4194304 | tf_op jit(solution)/shard_map/vmap()/dot_general | solution.py:26
  72.0 0.1 copy-done.6
  72.1 2.2 %fusion.6 = f32[2,512,512]{1,2,0:T(8,128)S(1)} fusion(bf16[2,512,512]{2,1,0:T(8,128)(2,1)S(1)} %copy-done.6, f32[2,512,512]{2,1,0:T(8,128)S(1)} %copy-done.4, f32[]{:T(128)S(6)} %mul.109, bf16[2,512,512]{2,0,1:T(2,128)(2,1)S(1)} %reshape.167), kind=kOutput, calls=%fused_computation.12 | convolution fusion | flops 3223322624 | bytes 6291460 | tf_op jit(solution)/shard_map/vmap()/dot_general | solution.py:33
  74.3 1.8 %fusion.48 = f32[2,512,512]{2,1,0:T(8,128)S(1)} fusion(f32[2,512,512]{1,2,0:T(8,128)S(1)} %fusion.6, bf16[2,512,512]{2,1,0:T(8,128)(2,1)S(1)} %copy-done), kind=kOutput, calls=%fused_computation.85 | convolution fusion | flops 3221225472 | bytes 5242880 | tf_op jit(solution)/shard_map/vmap()/dot_general | solution.py:32
  76.1 4.1 %broadcast_select_fusion = (f32[2,512,512]{2,1,0:T(8,128)}, f32[2,512,512]{2,1,0:T(8,128)}, f32[2,512,512]{2,1,0:T(8,128)S(1)}) fusion(f32[2,512,512]{2,1,0:T(8,128)S(1)} %copy-done.11, pred[2]{0:T(512)(128)(4,1)S(1)} %compare_reduce_fusion.2, f32[2,512,512]{2,1,0:T(8,128)S(1)} %copy-done.4, bf16[2,512,512]{2,0,1:T(2,128)(2,1)S(1)} %reshape.167, ...), kind=kOutput, calls=%fused_computation.31 | convolution fusion | flops 3226992640 | bytes 14680074 | tf_op jit(solution)/shard_map/vmap()/dot_general | solution.py:27
  80.2 2.6 %fusion.1 = f32[2,512,512]{1,2,0:T(8,128)S(1)} fusion(bf16[2,512,512]{2,1,0:T(8,128)(2,1)S(1)} %copy-done.6, f32[2,512,512]{2,1,0:T(8,128)S(1)} %fusion.48, f32[2,512,512]{2,1,0:T(8,128)S(1)} %get-tuple-element.36), kind=kOutput, calls=%fused_computation.6 | convolution fusion | flops 3222274048 | bytes 7340032 | tf_op jit(solution)/shard_map/vmap()/dot_general | solution.py:37
  82.8 1.9 %fusion.11 = bf16[2,512,512]{2,1,0:T(8,128)(2,1)S(1)} fusion(f32[2,512,512]{1,2,0:T(8,128)S(1)} %fusion.1, bf16[2,512,512]{2,1,0:T(8,128)(2,1)S(1)} %copy-done, pred[2]{0:T(512)(128)(4,1)S(1)} %compare_reduce_fusion.2), kind=kOutput, calls=%fused_computation.24 | convolution fusion | flops 3222274048 | bytes 4194306 | tf_op jit(solution)/shard_map/vmap()/dot_general | solution.py:36
  84.7 1.1 reshape.168
  85.8 2.0 %bitcast_convert_fusion = bf16[8,512,128]{2,0,1:T(8,128)(2,1)S(1)} fusion(bf16[2,512,4,128]{3,2,1,0:T(4,128)(2,1)} %reshape.168, s32[2,8]{1,0:T(2,128)S(1)} %broadcast_add_fusion, pred[2,8]{1,0:T(4,128)(4,1)S(1)} %get-tuple-element.31), kind=kOutput, calls=%fused_computation.2 | convolution fusion | flops 8913024 | bytes 2097232 | tf_op jit(solution)/shard_map/kjp,kbjt->pbt/dot_general | solution.py:114
  87.8 1.1 copy.96
  89.0 19.0 %all-to-all-done.2 = f32[8,64,896]{2,1,0:T(8,128)} async-done(((f32[8,64,896]{2,1,0:T(8,128)}), f32[8,64,896]{2,1,0:T(8,128)}, u32[]{:S(2)}, u32[]{:S(2)}) %all-to-all-start.2) | async-done | bytes 1835040 | tf_op jit(solution)/shard_map/all_to_all | solution.py:67
  107.9 3.8 %all-to-all-start.1 = ((bf16[8,512,128]{2,1,0:T(8,128)(2,1)}), bf16[8,512,128]{2,1,0:T(8,128)(2,1)S(1)}, u32[]{:S(2)}, u32[]{:S(2)}) async-start(bf16[8,512,128]{2,1,0:T(8,128)(2,1)} %copy.96), calls=%async_computation.1 | async-start | bytes 2097152 | tf_op jit(solution)/shard_map/all_to_all | solution.py:117
  111.7 2.7 %copy.99 = f32[512,896]{0,1:T(8,128)} copy(f32[512,896]{1,0:T(8,128)} %param.14) | data formatting | bytes 3670016 | tf_op args[3]
  114.5 0.2 convert_reduce_fusion
  114.7 0.2 fusion.26
  114.9 0.2 compare_reduce_fusion
  115.1 1.1 copy.101
  116.2 21.2 %all-to-all-done.1 = bf16[8,512,128]{2,1,0:T(8,128)(2,1)S(1)} async-done(((bf16[8,512,128]{2,1,0:T(8,128)(2,1)}), bf16[8,512,128]{2,1,0:T(8,128)(2,1)S(1)}, u32[]{:S(2)}, u32[]{:S(2)}) %all-to-all-start.1) | async-done | bytes 1048608 | tf_op jit(solution)/shard_map/all_to_all | solution.py:117
  137.4 4.2 %all-to-all-start.3 = ((bf16[2,8,64,512]{3,2,0,1:T(8,128)(2,1)}), bf16[2,8,64,512]{3,2,0,1:T(8,128)(2,1)}, u32[]{:S(2)}, u32[]{:S(2)}) async-start(bf16[2,8,64,512]{3,2,0,1:T(8,128)(2,1)} %copy.101), calls=%async_computation.3 | async-start | bytes 2097152 | tf_op jit(solution)/shard_map/all_to_all | solution.py:123
  141.8 3.9 %add_select_fusion.1 = f32[2,512,512]{2,1,0:T(8,128)} fusion(f32[2,512,512]{2,1,0:T(8,128)} %param.16, f32[]{:T(128)S(6)} %mul.131, pred[2]{0:T(512)(128)(4,1)S(1)} %compare_reduce_fusion.2, bf16[2,512,512]{2,0,1:T(2,128)(2,1)S(1)} %reshape.167), kind=kOutput, calls=%fused_computation.4 | convolution fusion | flops 538968064 | bytes 5242886 | tf_op jit(solution)/shard_map/vmap()/dot_general | solution.py:19
  145.7 2.1 %add_select_fusion = f32[2,512,512]{2,1,0:T(8,128)} fusion(f32[2,512,512]{2,1,0:T(8,128)S(1)} %copy-done.10, bf16[2,512,512]{1,2,0:T(8,128)(2,1)S(1)} %copy-done.3, f32[]{:T(128)S(6)} %mul.131, pred[2]{0:T(512)(128)(4,1)S(1)} %compare_reduce_fusion.2, bf16[2,512,512]{2,0,1:T(2,128)(2,1)S(1)} %reshape.167), kind=kOutput, calls=%fused_computation.3 | convolution fusion | flops 538968064 | bytes 6291462 | tf_op jit(solution)/shard_map/vmap()/dot_general | solution.py:20
  147.8 2.9 %copy.122 = f32[8,8,8,896]{3,2,0,1:T(8,128)} copy(f32[8,8,8,896]{3,2,1,0:T(8,128)} %bitcast.26) | data formatting | bytes 3670016 | tf_op jit(solution)/shard_map/all_to_all | solution.py:67
  150.8 0.8 multiply_bitcast_fusion
  151.6 1.7 copy.98
  153.3 2.5 %bitcast_subtract_fusion.1 = f32[512,896]{0,1:T(8,128)S(1)} fusion(f32[512,896]{0,1:T(8,128)} %copy.99, f32[512,7,128]{0,2,1:T(8,128)} %copy.98), kind=kLoop, calls=%fused_computation.18 | loop fusion | flops 458752 | bytes 5505024 | tf_op jit(solution)/shard_map/sub | solution.py:121
  155.7 1.7 copy.107
  157.4 9.8 %all-to-all-done.3 = bf16[2,8,64,512]{3,2,0,1:T(8,128)(2,1)} async-done(((bf16[2,8,64,512]{3,2,0,1:T(8,128)(2,1)}), bf16[2,8,64,512]{3,2,0,1:T(8,128)(2,1)}, u32[]{:S(2)}, u32[]{:S(2)}) %all-to-all-start.3) | async-done | bytes 1048608 | tf_op jit(solution)/shard_map/all_to_all | solution.py:123
  167.2 1.3 reshape.178
  168.6 0.7 bitcast_multiply_fusion
  169.3 0.8 copy-done.12
  170.1 1.9 %fusion.9 = f32[64,7168]{1,0:T(8,128)} fusion(f32[64,7168]{1,0:T(8,128)S(1)} %copy-done.12, f32[64,7168]{1,0:T(8,128)S(1)} %bitcast.73, f32[8,8,56,128]{3,2,1,0:T(8,128)S(1)} %bitcast.74), kind=kLoop, calls=%fused_computation.16 | loop fusion | flops 1835008 | bytes 7340032 | tf_op jit(solution)/shard_map/add | solution.py:142
  (37 shorter events, 0.4 us)
Async XLA Ops:
  0.6 73.6 %copy-start = (bf16[2,512,512]{2,1,0:T(8,128)(2,1)S(1)}, bf16[2,512,512]{2,1,0:T(8,128)(2,1)}, u32[]{:S(2)}) copy-start(bf16[2,512,512]{2,1,0:T(8,128)(2,1)} %param.19) | copy-start | bytes 3145732
  5.2 8.4 %copy-start.9 = (bf16[512,896]{1,0:T(8,128)(2,1)S(1)}, bf16[512,896]{1,0:T(8,128)(2,1)}, u32[]{:S(2)}) copy-start(bf16[512,896]{1,0:T(8,128)(2,1)} %param.11) | copy-start | bytes 2752516
  5.2 54.4 %copy-start.13 = (s32[56]{0:T(128)S(1)}, s32[56]{0:T(128)}, u32[]{:S(2)}) copy-start(s32[56]{0:T(128)} %param.12) | copy-start | bytes 676
  6.4 54.8 %all-to-all-start = ((bf16[8,512,128]{2,1,0:T(8,128)(2,1)}), bf16[8,512,128]{2,1,0:T(8,128)(2,1)S(1)}, u32[]{:S(2)}, u32[]{:S(2)}) async-start(bf16[8,512,128]{2,1,0:T(8,128)(2,1)} %copy.86), calls=%async_computation | async-start | bytes 2097152 | tf_op jit(solution)/shard_map/all_to_all | solution.py:86
  61.2 46.7 %all-to-all-start.2 = ((f32[8,64,896]{2,1,0:T(8,128)}), f32[8,64,896]{2,1,0:T(8,128)}, u32[]{:S(2)}, u32[]{:S(2)}) async-start(f32[8,64,896]{2,1,0:T(8,128)} %bitcast.11), calls=%async_computation.2 | async-start | bytes 3670016 | tf_op jit(solution)/shard_map/all_to_all | solution.py:67
  69.5 4.7 %copy-start.2 = (bf16[2,512,512]{1,2,0:T(8,128)(2,1)}, bf16[2,512,512]{1,2,0:T(8,128)(2,1)S(1)}, u32[]{:S(2)}) copy-start(bf16[2,512,512]{1,2,0:T(8,128)(2,1)S(1)} %copy.91) | copy-start | bytes 3145732
  69.5 2.4 %copy-start.4 = (f32[2,512,512]{2,1,0:T(8,128)S(1)}, f32[2,512,512]{2,1,0:T(8,128)}, u32[]{:S(2)}) copy-start(f32[2,512,512]{2,1,0:T(8,128)} %param.20) | copy-start | bytes 6291460
  69.5 2.5 %copy-start.6 = (bf16[2,512,512]{2,1,0:T(8,128)(2,1)S(1)}, bf16[2,512,512]{2,1,0:T(8,128)(2,1)}, u32[]{:S(2)}) copy-start(bf16[2,512,512]{2,1,0:T(8,128)(2,1)} %param.18) | copy-start | bytes 3145732
  74.3 1.9 %copy-start.11 = (f32[2,512,512]{2,1,0:T(8,128)S(1)}, f32[2,512,512]{2,1,0:T(8,128)}, u32[]{:S(2)}) copy-start(f32[2,512,512]{2,1,0:T(8,128)} %param.21) | copy-start | bytes 6291460
  107.9 29.5 %all-to-all-start.1 = ((bf16[8,512,128]{2,1,0:T(8,128)(2,1)}), bf16[8,512,128]{2,1,0:T(8,128)(2,1)S(1)}, u32[]{:S(2)}, u32[]{:S(2)}) async-start(bf16[8,512,128]{2,1,0:T(8,128)(2,1)} %copy.96), calls=%async_computation.1 | async-start | bytes 2097152 | tf_op jit(solution)/shard_map/all_to_all | solution.py:117
  137.4 4.3 %copy-start.7 = (bf16[8,512,128]{2,1,0:T(8,128)(2,1)}, bf16[8,512,128]{2,1,0:T(8,128)(2,1)S(1)}, u32[]{:S(2)}) copy-start(bf16[8,512,128]{2,1,0:T(8,128)(2,1)S(1)} %all-to-all-done.1) | copy-start | bytes 3145732
  137.4 29.8 %all-to-all-start.3 = ((bf16[2,8,64,512]{3,2,0,1:T(8,128)(2,1)}), bf16[2,8,64,512]{3,2,0,1:T(8,128)(2,1)}, u32[]{:S(2)}, u32[]{:S(2)}) async-start(bf16[2,8,64,512]{3,2,0,1:T(8,128)(2,1)} %copy.101), calls=%async_computation.3 | async-start | bytes 2097152 | tf_op jit(solution)/shard_map/all_to_all | solution.py:123
  141.8 3.9 %copy-start.3 = (bf16[2,512,512]{1,2,0:T(8,128)(2,1)S(1)}, bf16[2,512,512]{1,2,0:T(8,128)(2,1)}, u32[]{:S(2)}) copy-start(bf16[2,512,512]{1,2,0:T(8,128)(2,1)} %copy-done.2) | copy-start | bytes 3145732
  141.8 3.9 %copy-start.10 = (f32[2,512,512]{2,1,0:T(8,128)S(1)}, f32[2,512,512]{2,1,0:T(8,128)}, u32[]{:S(2)}) copy-start(f32[2,512,512]{2,1,0:T(8,128)} %param.17) | copy-start | bytes 6291460
  147.8 3.0 %copy-start.8 = (bf16[8,512,128]{2,1,0:T(8,128)(2,1)S(1)}, bf16[8,512,128]{2,1,0:T(8,128)(2,1)}, u32[]{:S(2)}) copy-start(bf16[8,512,128]{2,1,0:T(8,128)(2,1)} %copy-done.7) | copy-start | bytes 3145732
  157.4 11.9 %copy-start.5 = (f32[8,8,8,896]{3,2,0,1:T(8,128)S(1)}, f32[8,8,8,896]{3,2,0,1:T(8,128)}, u32[]{:S(2)}) copy-start(f32[8,8,8,896]{3,2,0,1:T(8,128)} %copy.122) | copy-start | bytes 5505028
  168.6 1.5 copy-start.12
  169.3 2.7 %copy-start.1 = (bf16[2,512,512]{2,1,0:T(8,128)(2,1)S(1)}, bf16[2,512,512]{2,1,0:T(8,128)(2,1)}, u32[]{:S(2)}) copy-start(bf16[2,512,512]{2,1,0:T(8,128)(2,1)} %param.19) | copy-start | bytes 3145732
where the time goes:
time: 173 us; the launch traced here: 172 us
  waiting for transfers between devices  50 us (29%)
  blocking collectives  44.9 us (26%)
  matrix products  25.9 us (15%)
  local copies, waits for them, and re-layouts  21.1 us (12%)
  starting transfers between devices  20.6 us (12%)
  other arithmetic  7.8 us (5%)
    psum x1, blocking collectives, on_device(): square_sum = lax.psum(jnp.sum(wide_grad * wide_grad), ('dp', 'tensor'))  44.9 us
    all_to_all x1, waiting for transfers between devices, on_device(): lax.all_to_all(backward, 'tensor', split_axis=0, concat_axis=0, tiled=True)  21.2 us
    all_to_all x1, waiting for transfers between devices, on_device(): lax.all_to_all(fast_weight, 'tensor', split_axis=0, concat_axis=1, tiled=...  19 us
    all_to_all x1, waiting for transfers between devices, on_device(): lax.all_to_all(rows_out, 'tensor', split_axis=1, concat_axis=1, tiled=True)  9.82 us
    all_to_all x1, starting transfers between devices, on_device(): lax.all_to_all(outgoing, 'tensor', split_axis=0, concat_axis=0, tiled=True)  7.25 us
    unnamed x31, local copies, waits for them, and re-layouts  6.86 us
    all_to_all x1, starting transfers between devices, on_device(): lax.all_to_all(fast_weight, 'tensor', split_axis=0, concat_axis=1, tiled=...  5.32 us
    all_to_all x1, starting transfers between devices, on_device(): lax.all_to_all(rows_out, 'tensor', split_axis=1, concat_axis=1, tiled=True)  4.23 us
  transfers between devices with their start and end apart: 4, of which 3 were waited for; matrix products, arithmetic and copies ran while one was open for 26% of the time, Pallas kernels for 0%

commit v1 on v0

v1 whole, which is shorter than its diff:
```python
import functools

import jax
import jax.numpy as jnp
from jax import lax
from jax.experimental import pallas as pl
from jax.experimental.pallas import tpu as pltpu
from jax.sharding import PartitionSpec as P

BETA_STAT = 0.95
BETA_ONE = 0.9
BETA_TWO = 0.95
ADAM_EPS = 1e-08
STEP_RATE = 0.1
PULL_RATE = 0.5
CLIP_RMS = 0.5
F32 = jnp.float32
BF16 = jnp.bfloat16
ANY = pl.BlockSpec(memory_space=pl.ANY)
SMEM = pl.BlockSpec(memory_space=pltpu.SMEM)


def mm(a, b):
    return jnp.dot(a, b, preferred_element_type=F32)


def mm_nt(a, b):
    return lax.dot_general(a, b, (((1,), (1,)), ((), ())), preferred_element_type=F32)


def halves(x):
    high = x.astype(BF16)
    return high, (x - high.astype(F32)).astype(BF16)


def body(
    sizes,
    owner_ref, tiles_ref, grad_hbm, fast_hbm, left_hbm, right_hbm, lbase_hbm, rbase_hbm, first_hbm, second_hbm,
    home_out, flat_out, left_out, right_out, first_out, second_out,
    gt, pack, recv, back, returned, pieces, rowsr, home, flat,
    fast_v, coded, coded_r, scale, scale_r,
    left_v, right_v, lbase, rbase, lbase_t, first_v, second_v, pre, gblk,
    part, tens_sum, dp_part, dp_sum, table,
    in_sems, grad_sems, out_sems, g_send, g_recv, f_send, f_recv, c_send, c_recv, b_send, b_recv, r_send, r_recv,
    s_send, s_recv, d_send, d_recv, own_sems,
):
    n_dp, n_t, slots, tile, shard_tiles, per_block, rows_flat, row_blocks, total = sizes
    t = lax.axis_index("tensor")
    dp = lax.axis_index("dp")

    def local(src, dst, sem):
        c = pltpu.make_async_copy(src, dst, sem)
        c.start()
        return c

    grad_in = [
        local(grad_hbm.at[:, pl.ds(i * tile, tile)], gt.at[i], grad_sems.at[i]) for i in range(shard_tiles)
    ]
    lb_in = local(lbase_hbm, lbase, in_sems.at[0])
    first_in = local(first_hbm, first_v, in_sems.at[1])
    rb_in = local(rbase_hbm, rbase, in_sems.at[2])
    second_in = local(second_hbm, second_v, in_sems.at[3])
    fast_in = local(fast_hbm, fast_v, in_sems.at[6])
    left_in = local(left_hbm, left_v, in_sems.at[4])
    right_in = local(right_hbm, right_v, in_sems.at[5])

    def to_t(d):
        return {"tensor": lax.rem(t + d, n_t)}

    def to_d(d):
        return {"dp": lax.rem(dp + d, n_dp)}

    barrier = pltpu.get_barrier_semaphore()
    for d in range(1, n_t):
        pl.semaphore_signal(barrier, inc=1, device_id=to_t(d), device_id_type=pl.DeviceIdType.MESH)
    for d in range(1, n_dp):
        pl.semaphore_signal(barrier, inc=1, device_id=to_d(d), device_id_type=pl.DeviceIdType.MESH)

    tb = [tiles_ref[dp, g] for g in range(n_t * shard_tiles)]
    my_owner = [
        lax.rem(owner_ref[tiles_ref[dp, t * shard_tiles + i]] // slots, n_t) for i in range(shard_tiles)
    ]
    send_tile = []
    for p in range(n_t):
        idx = jnp.int32(0)
        for i in range(shard_tiles):
            idx = jnp.where(my_owner[i] == p, i, idx)
        send_tile.append(idx)

    for c in grad_in:
        c.wait()

    def square(i, acc):
        wide = gt[i].astype(F32)
        return acc + jnp.sum((wide * wide).reshape(-1, 8, tile), axis=0)

    part[...] = lax.fori_loop(0, shard_tiles, square, jnp.zeros((8, tile), F32))
    for p in range(n_t):
        pack[p] = gt[send_tile[p]]
    pl.semaphore_wait(barrier, n_t + n_dp - 2)

    def remote(src, dst, ssem, rsem, to):
        return pltpu.make_async_remote_copy(
            src_ref=src, dst_ref=dst, send_sem=ssem, recv_sem=rsem, device_id=to,
            device_id_type=pl.DeviceIdType.MESH,
        )

    def peer(d):
        return lax.rem(t + d, n_t)

    def origin(d):
        return lax.rem(t + n_t - d, n_t)

    def sum_copy(d, slot):
        return remote(part, tens_sum.at[slot], s_send.at[d], s_recv.at[slot], to_t(d))

    def grad_copy(d, slot):
        return remote(pack.at[peer(d)], recv.at[slot], g_send.at[d], g_recv.at[slot], to_t(d))

    def code_copy(d, slot):
        return remote(coded.at[peer(d)], coded_r.at[slot], f_send.at[d], f_recv.at[slot], to_t(d))

    def scale_copy(d, slot):
        return remote(scale.at[peer(d)], scale_r.at[slot], c_send.at[d], c_recv.at[slot], to_t(d))

    def dp_copy(d, slot):
        return remote(dp_part, dp_sum.at[slot], d_send.at[d], d_recv.at[slot], to_d(d))

    def back_copy(d, slot):
        return remote(back.at[peer(d)], returned.at[slot], b_send.at[d], b_recv.at[slot], to_t(d))

    def rows_copy(d, k, slot):
        return remote(
            pieces.at[pl.ds(k * per_block, per_block), pl.ds(peer(d) * rows_flat, rows_flat), :],
            rowsr.at[pl.ds((slot * slots + k) * per_block, per_block)],
            r_send.at[k, d], r_recv.at[k, slot], to_t(d),
        )

    others = range(1, n_t)
    for d in others:
        sum_copy(d, t).start()
    for d in others:
        grad_copy(d, t).start()
    own_grad = local(pack.at[t], recv.at[t], own_sems.at[0])

    rank = []
    for a in range(n_t):
        count = jnp.int32(0)
        for b in range(a):
            same = tb[b * shard_tiles] == tb[a * shard_tiles]
            for i in range(1, shard_tiles):
                same = same | (tb[b * shard_tiles + i] == tb[a * shard_tiles])
            count = count + same.astype(jnp.int32)
        rank.append(count)
    present = []
    source = [jnp.int32(0)] * n_t
    for k in range(slots):
        block = jnp.int32(-1)
        slot_id = (dp * n_t + t) * slots + k
        for r in range(row_blocks):
            number = dp * row_blocks + r
            block = jnp.where(owner_ref[number] == slot_id, number, block)
        present.append(block >= 0)
        places = [jnp.int32(0)] * per_block
        for a in range(n_t):
            has = tb[a * shard_tiles] == block
            for i in range(1, shard_tiles):
                has = has | (tb[a * shard_tiles + i] == block)
            source[a] = jnp.where(has, k * per_block + rank[a], source[a])
            for j in range(per_block):
                places[j] = jnp.where(has & (rank[a] == j), a, places[j])
        for j in range(per_block):
            table[k * per_block + j] = places[j]
        table[slots * per_block + k] = (block >= 0).astype(jnp.int32)

    lb_in.wait()
    rb_in.wait()
    first_in.wait()

    def before(k, carry):
        turned = lbase[k].astype(F32).T.astype(BF16)
        lbase_t[k] = turned
        high, low = halves(first_v[k])
        high, low = halves(mm(turned, high) + mm(turned, low))
        pre[k] = BETA_ONE * (mm(high, rbase[k]) + mm(low, rbase[k]))
        return carry

    lax.fori_loop(0, slots, before, 0)

    fast_in.wait()

    def encode(p, carry):
        x = fast_v[pl.ds(pl.multiple_of(p * rows_flat, 16), rows_flat), :]
        top = jnp.maximum(jnp.max(jnp.abs(x), axis=1, keepdims=True), 1e-30)
        coded[p] = jnp.floor(x * (32767.0 / top) + 0.5).astype(jnp.int32).astype(jnp.int16)
        wide = jnp.broadcast_to(top * (1.0 / 32767.0), (rows_flat, tile))
        scale[p] = jnp.concatenate([wide] * (tile // rows_flat), axis=0).T[:8]
        return carry

    lax.fori_loop(0, n_t, encode, 0)

    for d in others:
        sum_copy(d, origin(d)).wait_recv()
    tens_sum[t] = part[...]
    dp_part[...] = jnp.sum(tens_sum[...], axis=0)
    for d in range(1, n_dp):
        dp_copy(d, dp).start()
    dp_sum[dp] = dp_part[...]
    for d in range(1, n_dp):
        dp_copy(d, lax.rem(dp + n_dp - d, n_dp)).wait_recv()
    square_sum = jnp.sum(jnp.sum(dp_sum[...], axis=0), axis=(0, 1), keepdims=True)
    factor = CLIP_RMS / jnp.sqrt(square_sum / total + 1e-06)

    for d in others:
        grad_copy(d, t).wait_send()
    for d in others:
        code_copy(d, t).start()
        scale_copy(d, t).start()
    coded_r[t] = coded[t]
    scale_r[t] = scale[t]
    own_grad.wait()
    for d in others:
        grad_copy(d, origin(d)).wait_recv()
    second_in.wait()

    def main(k, carry):
        for j in range(per_block):
            gblk[k, :, j * tile : (j + 1) * tile] = recv[table[k * per_block + j]]
        there = table[slots * per_block + k] > 0
        g = gblk[k]
        high, low = halves(mm(lbase_t[k], g))
        rotated = factor * (mm(high, rbase[k]) + mm(low, rbase[k]))
        fresh = BETA_TWO * second_v[k] + (1.0 - BETA_TWO) * rotated * rotated
        second_v[k] = jnp.where(there, fresh, second_v[k])
        direction = (pre[k] + (1.0 - BETA_ONE) * rotated) / (jnp.sqrt(fresh) + ADAM_EPS)
        high, low = halves(direction)
        high, low = halves(mm(lbase[k], high) + mm(lbase[k], low))
        update = (mm_nt(high, rbase[k]) + mm_nt(low, rbase[k])).astype(BF16)
        for j in range(per_block):
            pieces[k * per_block + j] = update[:, j * tile : (j + 1) * tile]
        return carry

    lax.fori_loop(0, slots, main, 0)
    for p in range(n_t):
        back[p] = pieces[source[p]]
    for d in others:
        back_copy(d, t).start()
    for k in range(slots):
        for d in others:
            rows_copy(d, k, t).start()
    own_back = local(back.at[t], returned.at[t], own_sems.at[2])
    own_rows = [
        local(
            pieces.at[pl.ds(k * per_block, per_block), pl.ds(t * rows_flat, rows_flat), :],
            rowsr.at[pl.ds((t * slots + k) * per_block, per_block)],
            own_sems.at[3 + k],
        )
        for k in range(slots)
    ]

    left_in.wait()
    right_in.wait()
    squared = (1.0 - BETA_STAT) * (factor * factor)

    def after(k, carry):
        there = table[slots * per_block + k] > 0
        g = gblk[k]
        wide = g.astype(F32)
        turned = wide.T.astype(BF16)
        left_v[k] = jnp.where(there, BETA_STAT * left_v[k] + squared * mm_nt(g, g), left_v[k])
        right_v[k] = jnp.where(there, BETA_STAT * right_v[k] + squared * mm(turned, g), right_v[k])
        first_v[k] = jnp.where(
            there, BETA_ONE * first_v[k] + ((1.0 - BETA_ONE) * factor) * wide, first_v[k]
        )
        return carry

    second_done = local(second_v, second_out, out_sems.at[0])
    lax.fori_loop(0, slots, after, 0)
    done = [
        second_done,
        local(left_v, left_out, out_sems.at[1]),
        local(right_v, right_out, out_sems.at[2]),
        local(first_v, first_out, out_sems.at[3]),
    ]

    for d in others:
        code_copy(d, origin(d)).wait_recv()
        scale_copy(d, origin(d)).wait_recv()
    for a in range(n_t):
        step = jnp.broadcast_to(scale_r[a, 0:1, :], (tile, tile)).T[:rows_flat]
        for i in range(shard_tiles):
            g = a * shard_tiles + i
            words = coded_r[a, :, i * tile : (i + 1) * tile].astype(jnp.int32)
            flat[:, g * tile : (g + 1) * tile] = words.astype(F32) * step
    own_back.wait()
    for d in others:
        back_copy(d, origin(d)).wait_recv()
    for i in range(shard_tiles):
        home[:, i * tile : (i + 1) * tile] = returned[my_owner[i]]
    done.append(local(home, home_out, out_sems.at[4]))
    for c in own_rows:
        c.wait()
    for k in range(slots):
        for d in others:
            rows_copy(d, k, origin(d)).wait_recv()
    for a in range(n_t):
        for i in range(shard_tiles):
            g = a * shard_tiles + i
            place = lax.rem(owner_ref[tb[g]], n_t * slots) * per_block + rank[a]
            at = slice(g * tile, (g + 1) * tile)
            flat[:, at] = flat[:, at] - STEP_RATE * rowsr[place].astype(F32)
    done.append(local(flat, flat_out, out_sems.at[5]))
    for d in others:
        sum_copy(d, t).wait_send()
        code_copy(d, t).wait_send()
        scale_copy(d, t).wait_send()
        back_copy(d, t).wait_send()
        for k in range(slots):
            rows_copy(d, k, t).wait_send()
    for d in range(1, n_dp):
        dp_copy(d, dp).wait_send()
    for c in done:
        c.wait()


def on_device(
    gradient, block_owner, tile_block, fast_weight, slow_flat,
    left_stat, right_stat, left_basis, right_basis, first_moment, second_moment,
):
    block = left_stat.shape[1]
    slots = left_stat.shape[0]
    rows, shard_cols = gradient.shape
    n_t = lax.axis_size("tensor")
    n_dp = lax.axis_size("dp")
    tile_count = tile_block.shape[1]
    cols = shard_cols * n_t
    tile = cols // tile_count
    shard_tiles = shard_cols // tile
    per_block = block // tile
    rows_flat = block // n_t
    row_blocks = block_owner.shape[0] // n_dp
    sizes = (n_dp, n_t, slots, tile, shard_tiles, per_block, rows_flat, row_blocks, rows * cols * n_dp)
    vm = pltpu.VMEM
    dma = pltpu.SemaphoreType.DMA
    big = (slots, block, block)
    stripes = (n_t, block, tile)
    out = jax.ShapeDtypeStruct
    home, flat, left_new, right_new, first_new, second_new = pl.pallas_call(
        functools.partial(body, sizes),
        out_shape=(
            out((rows, shard_cols), BF16),
            out((rows_flat, cols), F32),
            out(big, F32), out(big, F32), out(big, F32), out(big, F32),
        ),
        in_specs=[SMEM, SMEM] + [ANY] * 8,
        out_specs=(ANY,) * 6,
        scratch_shapes=[
            vm((shard_tiles, block, tile), BF16),
            vm(stripes, BF16), vm(stripes, BF16), vm(stripes, BF16), vm(stripes, BF16),
            vm((slots * per_block, block, tile), BF16),
            vm((n_t * slots * per_block, rows_flat, tile), BF16),
            vm((rows, shard_cols), BF16), vm((rows_flat, cols), F32),
            vm((rows, shard_cols), F32),
            vm((n_t, rows_flat, shard_cols), jnp.int16), vm((n_t, rows_flat, shard_cols), jnp.int16),
            vm((n_t, 8, tile), F32), vm((n_t, 8, tile), F32),
            vm(big, F32), vm(big, F32), vm(big, BF16), vm(big, BF16), vm(big, BF16),
            vm(big, F32), vm(big, F32), vm(big, F32), vm(big, BF16),
            vm((8, tile), F32), vm((n_t, 8, tile), F32), vm((8, tile), F32), vm((n_dp, 8, tile), F32),
            pltpu.SMEM((slots * (per_block + 1),), jnp.int32),
            dma((7,)), dma((shard_tiles,)), dma((6,)),
            dma((n_t,)), dma((n_t,)), dma((n_t,)), dma((n_t,)), dma((n_t,)), dma((n_t,)), dma((n_t,)), dma((n_t,)),
            dma((slots, n_t)), dma((slots, n_t)),
            dma((n_t,)), dma((n_t,)), dma((n_dp,)), dma((n_dp,)), dma((3 + slots,)),
        ],
        compiler_params=pltpu.CompilerParams(
            collective_id=0, has_side_effects=True, vmem_limit_bytes=56 * 2**20
        ),
    )(
        block_owner, tile_block, gradient, fast_weight, left_stat, right_stat, left_basis, right_basis,
        first_moment, second_moment,
    )
    fast_new = fast_weight - STEP_RATE * home.astype(F32)
    slow_new = slow_flat + PULL_RATE * (flat - slow_flat)
    return (fast_new, slow_new, left_new, right_new, first_new, second_new)


def solution(mesh):
    square = P("dp", "tensor")
    spread = P(("dp", "tensor"), None)
    slot = P(("dp", "tensor"), None, None)
    return jax.shard_map(
        on_device,
        mesh=mesh,
        in_specs=(square, P(), P(), square, spread) + (slot,) * 6,
        out_specs=(square, spread) + (slot,) * 4,
        check_vma=False,
    )
```

time: 173 us -> 114 us (0.66)
  Pallas kernels: 0 us -> 99.8 us
  waiting for transfers between devices: 50 us -> 0 us
  blocking collectives: 44.9 us -> 0 us
  matrix products: 25.9 us -> 0 us
  starting transfers between devices: 20.6 us -> 0 us
  local copies, waits for them, and re-layouts: 21.1 us -> 9.19 us
  other arithmetic: 7.8 us -> 4.5 us
    pallas_call x0 -> x1, Pallas kernels: none -> 99.8 us  [on_device(): pl.pallas_call(functools.partial(body, sizes), out_shape=(out((rows, shar...]
    all_to_all x4 -> x0, waiting for transfers between devices: 50 us -> none  [the longest x1 21.2 us: on_device(): lax.all_to_all(backward, 'tensor', split_axis=0, concat_axis=0, tiled=True)]
    psum x1 -> x0, blocking collectives: 44.9 us -> none  [on_device(): square_sum = lax.psum(jnp.sum(wide_grad * wide_grad), ('dp', 'tensor'))]
    dot_general x13 -> x0, matrix products: 25.9 us -> none  [the longest x1 4.09 us: soap_block(): rotated = factor * jnp.dot(half_rotated, right_wide, precision=HIGHEST)]
    all_to_all x4 -> x0, starting transfers between devices: 20.6 us -> none  [the longest x1 7.25 us: on_device(): lax.all_to_all(outgoing, 'tensor', split_axis=0, concat_axis=0, tiled=True)]
    reshape x6 -> x0, local copies, waits for them, and re-layouts: 6.41 us -> none  [the longest x2 2.07 us: on_device(): blocks = blocks.reshape(slot_count, block_size, block_size)]
    all_to_all x1 -> x0, local copies, waits for them, and re-layouts: 2.95 us -> none  [on_device(): lax.all_to_all(fast_weight, 'tensor', split_axis=0, concat_axis=1, tiled=...]
    reduce_sum x5 -> x0, other arithmetic: 2.48 us -> none  [the longest x1 1.07 us: on_device(): square_sum = lax.psum(jnp.sum(wide_grad * wide_grad), ('dp', 'tensor'))]
  transfers between devices with their start and end apart: 4 -> 0, of which waited for: 3 -> 0; matrix products, arithmetic and copies ran while one was open for 26% -> 0% of each run, Pallas kernels for 0% -> 0%
where the time goes in v1:
time: 114 us
  Pallas kernels  99.8 us (88%)
  local copies, waits for them, and re-layouts  9.19 us (8%)
  other arithmetic  4.5 us (4%)
    pallas_call x1, Pallas kernels, on_device(): pl.pallas_call(functools.partial(body, sizes), out_shape=(out((rows, shar...  99.8 us
    unnamed x18, local copies, waits for them, and re-layouts  9.19 us
    add x1, other arithmetic, on_device(): slow_new = slow_flat + PULL_RATE * (flat - slow_flat)  3.07 us

profile of v1, /device:TPU:0, one launch (start us, length us, event | category | flops | bytes accessed | tf_op | source)
XLA Modules:
  0.0 114.2 jit_solution(2806926489681132626)
XLA Ops:
  0.6 0.0 copy-start.5
  0.6 99.8 %shard_map.154 = (bf16[512,896]{1,0:T(8,128)(2,1)}, f32[64,7168]{1,0:T(8,128)}, f32[2,512,512]{2,1,0:T(8,128)}, f32[2,512,512]{2,1,0:T(8,128)}, f32[2,512,512]{2,1,0:T(8,128)}, /*index=5*/f32[2,512,512]{2,1,0:T(8,128)}) custom-call(s32[56]{0:T(128)} %owner_ref.1, s32[4,56]{1,0:T(4,128)} %tiles_ref.1, bf16[512,896]{1,0:T(8,128)(2,1)} %grad_hbm.1, ...), custom_call_target="tpu_custom_call" | custom-call | tf_op jit(solution)/shard_map/pallas_call | solution.py:348
  100.4 0.0 copy-done.5
  100.5 0.0 copy-start
  100.5 0.0 copy-start.6
  100.5 3.1 %multiply_add_fusion = f32[64,7168]{1,0:T(8,128)} fusion(f32[64,7168]{1,0:T(8,128)S(1)} %copy-done.5, f32[64,7168]{1,0:T(8,128)} %get-tuple-element.13), kind=kLoop, calls=%fused_computation | loop fusion | flops 1376256 | bytes 5505024 | tf_op jit(solution)/shard_map/add | solution.py:383
  103.5 0.0 copy-done
  103.5 0.0 copy-done.6
  103.6 0.0 copy-start.4
  103.6 1.4 %multiply_subtract_fusion = f32[512,896]{1,0:T(8,128)} fusion(f32[512,896]{1,0:T(8,128)S(1)} %copy-done, bf16[512,896]{1,0:T(8,128)(2,1)S(1)} %copy-done.6), kind=kLoop, calls=%fused_computation.1 | loop fusion | flops 1376256 | bytes 4587520 | tf_op jit(solution)/shard_map/sub | solution.py:382
  105.0 0.8 copy-done.4
  105.8 0.0 copy-start.3
  105.8 1.3 %copy.21 = f32[2,512,512]{2,1,0:T(8,128)} copy(f32[2,512,512]{2,1,0:T(8,128)S(1)} %copy-done.4) | data formatting | bytes 4194304
  107.1 1.0 copy-done.3
  108.2 0.0 copy-start.2
  108.2 1.3 %copy.22 = f32[2,512,512]{2,1,0:T(8,128)} copy(f32[2,512,512]{2,1,0:T(8,128)S(1)} %copy-done.3) | data formatting | bytes 4194304
  109.5 1.0 copy-done.2
  110.5 0.0 copy-start.1
  110.5 1.3 %copy.23 = f32[2,512,512]{2,1,0:T(8,128)} copy(f32[2,512,512]{2,1,0:T(8,128)S(1)} %copy-done.2) | data formatting | bytes 4194304
  111.8 1.0 copy-done.1
  112.9 1.3 %copy.24 = f32[2,512,512]{2,1,0:T(8,128)} copy(f32[2,512,512]{2,1,0:T(8,128)S(1)} %copy-done.1) | data formatting | bytes 4194304
Async XLA Ops:
  0.6 99.8 %copy-start.5 = (f32[64,7168]{1,0:T(8,128)S(1)}, f32[64,7168]{1,0:T(8,128)}, u32[]{:S(2)}) copy-start(f32[64,7168]{1,0:T(8,128)} %param.15) | copy-start | bytes 5505028
  100.5 3.1 %copy-start = (f32[512,896]{1,0:T(8,128)S(1)}, f32[512,896]{1,0:T(8,128)}, u32[]{:S(2)}) copy-start(f32[512,896]{1,0:T(8,128)} %fast_hbm.1) | copy-start | bytes 5505028
  100.5 3.1 %copy-start.6 = (bf16[512,896]{1,0:T(8,128)(2,1)S(1)}, bf16[512,896]{1,0:T(8,128)(2,1)}, u32[]{:S(2)}) copy-start(bf16[512,896]{1,0:T(8,128)(2,1)} %get-tuple-element.12) | copy-start | bytes 2752516
  103.6 2.3 %copy-start.4 = (f32[2,512,512]{2,1,0:T(8,128)S(1)}, f32[2,512,512]{2,1,0:T(8,128)}, u32[]{:S(2)}) copy-start(f32[2,512,512]{2,1,0:T(8,128)} %get-tuple-element.26) | copy-start | bytes 6291460
  105.8 2.3 %copy-start.3 = (f32[2,512,512]{2,1,0:T(8,128)S(1)}, f32[2,512,512]{2,1,0:T(8,128)}, u32[]{:S(2)}) copy-start(f32[2,512,512]{2,1,0:T(8,128)} %get-tuple-element.27) | copy-start | bytes 6291460
  108.2 2.3 %copy-start.2 = (f32[2,512,512]{2,1,0:T(8,128)S(1)}, f32[2,512,512]{2,1,0:T(8,128)}, u32[]{:S(2)}) copy-start(f32[2,512,512]{2,1,0:T(8,128)} %get-tuple-element.28) | copy-start | bytes 6291460
  110.5 2.3 %copy-start.1 = (f32[2,512,512]{2,1,0:T(8,128)S(1)}, f32[2,512,512]{2,1,0:T(8,128)}, u32[]{:S(2)}) copy-start(f32[2,512,512]{2,1,0:T(8,128)} %get-tuple-element.29) | copy-start | bytes 6291460

commit v2 on v1

--- a/solution.py
+++ b/solution.py
@@ -36,12 +36,11 @@
 def body(
     sizes,
     owner_ref, tiles_ref, grad_hbm, fast_hbm, left_hbm, right_hbm, lbase_hbm, rbase_hbm, first_hbm, second_hbm,
-    home_out, flat_out, left_out, right_out, first_out, second_out,
-    gt, pack, recv, back, returned, pieces, rowsr, home, flat,
-    fast_v, coded, coded_r, scale, scale_r,
+    fast_out, coded_out, scale_out, left_out, right_out, first_out, second_out,
+    gt, pack, recv, back, returned, pieces, fast_v, coded, scale,
     left_v, right_v, lbase, rbase, lbase_t, first_v, second_v, pre, gblk,
     part, tens_sum, dp_part, dp_sum, table,
-    in_sems, grad_sems, out_sems, g_send, g_recv, f_send, f_recv, c_send, c_recv, b_send, b_recv, r_send, r_recv,
+    in_sems, grad_sems, out_sems, g_send, g_recv, f_send, f_recv, c_send, c_recv, b_send, b_recv,
     s_send, s_recv, d_send, d_recv, own_sems,
 ):
     n_dp, n_t, slots, tile, shard_tiles, per_block, rows_flat, row_blocks, total = sizes
@@ -118,23 +117,16 @@
         return remote(pack.at[peer(d)], recv.at[slot], g_send.at[d], g_recv.at[slot], to_t(d))
 
     def code_copy(d, slot):
-        return remote(coded.at[peer(d)], coded_r.at[slot], f_send.at[d], f_recv.at[slot], to_t(d))
+        return remote(coded.at[peer(d)], coded_out.at[slot], f_send.at[d], f_recv.at[slot], to_t(d))
 
     def scale_copy(d, slot):
-        return remote(scale.at[peer(d)], scale_r.at[slot], c_send.at[d], c_recv.at[slot], to_t(d))
+        return remote(scale.at[peer(d)], scale_out.at[slot], c_send.at[d], c_recv.at[slot], to_t(d))
 
     def dp_copy(d, slot):
         return remote(dp_part, dp_sum.at[slot], d_send.at[d], d_recv.at[slot], to_d(d))
 
     def back_copy(d, slot):
         return remote(back.at[peer(d)], returned.at[slot], b_send.at[d], b_recv.at[slot], to_t(d))
-
-    def rows_copy(d, k, slot):
-        return remote(
-            pieces.at[pl.ds(k * per_block, per_block), pl.ds(peer(d) * rows_flat, rows_flat), :],
-            rowsr.at[pl.ds((slot * slots + k) * per_block, per_block)],
-            r_send.at[k, d], r_recv.at[k, slot], to_t(d),
-        )
 
     others = range(1, n_t)
     for d in others:
@@ -187,18 +179,6 @@
 
     lax.fori_loop(0, slots, before, 0)
 
-    fast_in.wait()
-
-    def encode(p, carry):
-        x = fast_v[pl.ds(pl.multiple_of(p * rows_flat, 16), rows_flat), :]
-        top = jnp.maximum(jnp.max(jnp.abs(x), axis=1, keepdims=True), 1e-30)
-        coded[p] = jnp.floor(x * (32767.0 / top) + 0.5).astype(jnp.int32).astype(jnp.int16)
-        wide = jnp.broadcast_to(top * (1.0 / 32767.0), (rows_flat, tile))
-        scale[p] = jnp.concatenate([wide] * (tile // rows_flat), axis=0).T[:8]
-        return carry
-
-    lax.fori_loop(0, n_t, encode, 0)
-
     for d in others:
         sum_copy(d, origin(d)).wait_recv()
     tens_sum[t] = part[...]
@@ -213,11 +193,6 @@
 
     for d in others:
         grad_copy(d, t).wait_send()
-    for d in others:
-        code_copy(d, t).start()
-        scale_copy(d, t).start()
-    coded_r[t] = coded[t]
-    scale_r[t] = scale[t]
     own_grad.wait()
     for d in others:
         grad_copy(d, origin(d)).wait_recv()
@@ -245,19 +220,7 @@
         back[p] = pieces[source[p]]
     for d in others:
         back_copy(d, t).start()
-    for k in range(slots):
-        for d in others:
-            rows_copy(d, k, t).start()
     own_back = local(back.at[t], returned.at[t], own_sems.at[2])
-    own_rows = [
-        local(
-            pieces.at[pl.ds(k * per_block, per_block), pl.ds(t * rows_flat, rows_flat), :],
-            rowsr.at[pl.ds((t * slots + k) * per_block, per_block)],
-            own_sems.at[3 + k],
-        )
-        for k in range(slots)
-    ]
-
     left_in.wait()
     right_in.wait()
     squared = (1.0 - BETA_STAT) * (factor * factor)
@@ -283,43 +246,84 @@
         local(first_v, first_out, out_sems.at[3]),
     ]
 
-    for d in others:
+    fast_in.wait()
+    own_back.wait()
+    for d in others:
+        back_copy(d, origin(d)).wait_recv()
+
+    def encode(d):
+        at = pl.ds(pl.multiple_of(peer(d) * rows_flat, rows_flat), rows_flat)
+        for i in range(shard_tiles):
+            lanes = slice(i * tile, (i + 1) * tile)
+            fast_v[at, lanes] = fast_v[at, lanes] - STEP_RATE * returned[my_owner[i], at, :].astype(F32)
+        x = fast_v[at, :]
+        top = jnp.maximum(jnp.max(jnp.abs(x), axis=1, keepdims=True), 1e-30)
+        coded[peer(d)] = jnp.floor(x * (32767.0 / top) + 0.5).astype(jnp.int32).astype(jnp.int16)
+        wide = jnp.broadcast_to(top * (1.0 / 32767.0), (rows_flat, tile))
+        scale[peer(d)] = jnp.concatenate([wide] * (tile // rows_flat), axis=0).T[:8]
+
+    for d in others:
+        encode(d)
+        code_copy(d, t).start()
+        scale_copy(d, t).start()
+    encode(0)
+    done += [
+        local(coded.at[t], coded_out.at[t], own_sems.at[1]),
+        local(scale.at[t], scale_out.at[t], own_sems.at[3]),
+        local(fast_v, fast_out, out_sems.at[4]),
+    ]
+    for d in others:
+        sum_copy(d, t).wait_send()
+        back_copy(d, t).wait_send()
+    for d in range(1, n_dp):
+        dp_copy(d, dp).wait_send()
+    for d in others:
+        code_copy(d, t).wait_send()
+        scale_copy(d, t).wait_send()
         code_copy(d, origin(d)).wait_recv()
         scale_copy(d, origin(d)).wait_recv()
+    for c in done:
+        c.wait()
+
+
+def finish(coded_hbm, scale_hbm, slow_hbm, *refs):
+    sources, slow_out, targets = refs[:5], refs[5], refs[6:11]
+    coded, scale, slow = refs[11:14]
+    held, in_sems, put_sems, sems = refs[14:19], refs[19], refs[20], refs[21]
+    n_t, rows_flat, width = coded.shape
+    tile = scale.shape[2]
+
+    def local(src, dst, sem):
+        c = pltpu.make_async_copy(src, dst, sem)
+        c.start()
+        return c
+
+    first = [
+        local(coded_hbm, coded, sems.at[0]),
+        local(scale_hbm, scale, sems.at[1]),
+        local(slow_hbm, slow, sems.at[2]),
+    ]
+    parts = [(n, h) for n in range(5) for h in range(2)]
+
+    def half(ref, h):
+        size = ref.shape[0] // 2
+        return ref.at[pl.ds(h * size, size)]
+
+    loads = [local(half(sources[n], h), half(held[n], h), in_sems.at[n, h]) for n, h in parts]
+    for c in first:
+        c.wait()
+    puts = []
     for a in range(n_t):
-        step = jnp.broadcast_to(scale_r[a, 0:1, :], (tile, tile)).T[:rows_flat]
-        for i in range(shard_tiles):
-            g = a * shard_tiles + i
-            words = coded_r[a, :, i * tile : (i + 1) * tile].astype(jnp.int32)
-            flat[:, g * tile : (g + 1) * tile] = words.astype(F32) * step
-    own_back.wait()
-    for d in others:
-        back_copy(d, origin(d)).wait_recv()
-    for i in range(shard_tiles):
-        home[:, i * tile : (i + 1) * tile] = returned[my_owner[i]]
-    done.append(local(home, home_out, out_sems.at[4]))
-    for c in own_rows:
+        step = jnp.broadcast_to(scale[a, 0:1, :], (tile, tile)).T[:rows_flat]
+        for i in range(width // tile):
+            words = coded[a, :, i * tile : (i + 1) * tile].astype(jnp.int32)
+            at = slice(a * width + i * tile, a * width + (i + 1) * tile)
+            slow[:, at] = slow[:, at] + PULL_RATE * (words.astype(F32) * step - slow[:, at])
+    puts.append(local(slow, slow_out, sems.at[3]))
+    for (n, h), c in zip(parts, loads):
         c.wait()
-    for k in range(slots):
-        for d in others:
-            rows_copy(d, k, origin(d)).wait_recv()
-    for a in range(n_t):
-        for i in range(shard_tiles):
-            g = a * shard_tiles + i
-            place = lax.rem(owner_ref[tb[g]], n_t * slots) * per_block + rank[a]
-            at = slice(g * tile, (g + 1) * tile)
-            flat[:, at] = flat[:, at] - STEP_RATE * rowsr[place].astype(F32)
-    done.append(local(flat, flat_out, out_sems.at[5]))
-    for d in others:
-        sum_copy(d, t).wait_send()
-        code_copy(d, t).wait_send()
-        scale_copy(d, t).wait_send()
-        back_copy(d, t).wait_send()
-        for k in range(slots):
-            rows_copy(d, k, t).wait_send()
-    for d in range(1, n_dp):
-        dp_copy(d, dp).wait_send()
-    for c in done:
+        puts.append(local(half(held[n], h), half(targets[n], h), put_sems.at[n, h]))
+    for c in puts:
         c.wait()
 
 
@@ -345,32 +349,28 @@
     big = (slots, block, block)
     stripes = (n_t, block, tile)
     out = jax.ShapeDtypeStruct
-    home, flat, left_new, right_new, first_new, second_new = pl.pallas_call(
+    fast_new, coded, scale, left_new, right_new, first_new, second_new = pl.pallas_call(
         functools.partial(body, sizes),
         out_shape=(
-            out((rows, shard_cols), BF16),
-            out((rows_flat, cols), F32),
+            out((rows, shard_cols), F32),
+            out((n_t, rows_flat, shard_cols), jnp.int16),
+            out((n_t, 8, tile), F32),
             out(big, F32), out(big, F32), out(big, F32), out(big, F32),
         ),
         in_specs=[SMEM, SMEM] + [ANY] * 8,
-        out_specs=(ANY,) * 6,
+        out_specs=(ANY,) * 7,
         scratch_shapes=[
             vm((shard_tiles, block, tile), BF16),
             vm(stripes, BF16), vm(stripes, BF16), vm(stripes, BF16), vm(stripes, BF16),
             vm((slots * per_block, block, tile), BF16),
-            vm((n_t * slots * per_block, rows_flat, tile), BF16),
-            vm((rows, shard_cols), BF16), vm((rows_flat, cols), F32),
-            vm((rows, shard_cols), F32),
-            vm((n_t, rows_flat, shard_cols), jnp.int16), vm((n_t, rows_flat, shard_cols), jnp.int16),
-            vm((n_t, 8, tile), F32), vm((n_t, 8, tile), F32),
+            vm((rows, shard_cols), F32), vm((n_t, rows_flat, shard_cols), jnp.int16), vm((n_t, 8, tile), F32),
             vm(big, F32), vm(big, F32), vm(big, BF16), vm(big, BF16), vm(big, BF16),
             vm(big, F32), vm(big, F32), vm(big, F32), vm(big, BF16),
             vm((8, tile), F32), vm((n_t, 8, tile), F32), vm((8, tile), F32), vm((n_dp, 8, tile), F32),
             pltpu.SMEM((slots * (per_block + 1),), jnp.int32),
             dma((7,)), dma((shard_tiles,)), dma((6,)),
             dma((n_t,)), dma((n_t,)), dma((n_t,)), dma((n_t,)), dma((n_t,)), dma((n_t,)), dma((n_t,)), dma((n_t,)),
-            dma((slots, n_t)), dma((slots, n_t)),
-            dma((n_t,)), dma((n_t,)), dma((n_dp,)), dma((n_dp,)), dma((3 + slots,)),
+            dma((n_t,)), dma((n_t,)), dma((n_dp,)), dma((n_dp,)), dma((4,)),
         ],
         compiler_params=pltpu.CompilerParams(
             collective_id=0, has_side_effects=True, vmem_limit_bytes=56 * 2**20
@@ -379,8 +379,18 @@
         block_owner, tile_block, gradient, fast_weight, left_stat, right_stat, left_basis, right_basis,
         first_moment, second_moment,
     )
-    fast_new = fast_weight - STEP_RATE * home.astype(F32)
-    slow_new = slow_flat + PULL_RATE * (flat - slow_flat)
+    states = (fast_new, left_new, right_new, first_new, second_new)
+    slow_new, *states = pl.pallas_call(
+        finish,
+        out_shape=tuple(out(a.shape, F32) for a in (slow_flat,) + states),
+        in_specs=[ANY] * 8,
+        out_specs=(ANY,) * 6,
+        scratch_shapes=[vm(coded.shape, jnp.int16), vm(scale.shape, F32), vm(slow_flat.shape, F32)]
+        + [vm(a.shape, F32) for a in states]
+        + [dma((5, 2)), dma((5, 2)), dma((4,))],
+        compiler_params=pltpu.CompilerParams(vmem_limit_bytes=56 * 2**20),
+    )(coded, scale, slow_flat, *states)
+    fast_new, left_new, right_new, first_new, second_new = states
     return (fast_new, slow_new, left_new, right_new, first_new, second_new)
 
 

time: 114 us -> 91.1 us (0.80)
  the two profiles are of different devices: /device:TPU:0 before, /device:TPU:26 now
where the time goes in v2:
time: 91.1 us; the launch traced here: 91 us
  Pallas kernels  90.3 us (99%)
    pallas_call x1, Pallas kernels, on_device(): pl.pallas_call(functools.partial(body, sizes), out_shape=(out((rows, shar...  80.8 us
    pallas_call x1, Pallas kernels, on_device(): pl.pallas_call(finish, out_shape=tuple((out(a.shape, F32) for a in (slow_...  9.53 us

profile of v2, /device:TPU:26, one launch (start us, length us, event | category | flops | bytes accessed | tf_op | source)
XLA Modules:
  0.0 91.0 jit_solution(2895991922156486695)
XLA Ops:
  0.6 80.8 %shard_map.154 = (f32[512,896]{1,0:T(8,128)}, s16[8,64,896]{2,1,0:T(8,128)(2,1)}, f32[8,8,128]{2,1,0:T(8,128)}, f32[2,512,512]{2,1,0:T(8,128)}, f32[2,512,512]{2...) custom-call(s32[56]{0:T(128)} %owner_ref.1, s32[4,56]{1,0:T(4,128)} %tiles_ref.1, ...), custom_call_target="tpu_custom_call" | custom-call | tf_op jit(solution)/shard_map/pallas_call | solution.py:352
  81.4 9.5 %shard_map.155 = (f32[64,7168]{1,0:T(8,128)}, f32[512,896]{1,0:T(8,128)}, f32[2,512,512]{2,1,0:T(8,128)}, f32[2,512,512]{2,1,0:T(8,128)}, f32[2,512,512]{2,1,0:T(8,128)}, /*index=5*/f32[2,512,512]{2,1,0:T(8,128)}) custom-call(s16[8,64,896]{2,1,0:T(8,128)(2,1)} %get-tuple-element.19.coded_hbm, f32[8,8,128]{2,1,0:T(8,128)} %get-tuple-element.20.scale_hbm, ...), custom_call_target="tpu_custom_call" | custom-call | tf_op jit(solution)/shard_map/pallas_call | solution.py:383
